TPU v7x, 32 devices: a whole 2x2x4 slice. The times are simulated.
32 devices in a mesh: days: 2 (over x), sta: 16 (over z, y, core).
Axes of the slice: x: 2, y: 2, z: 4, core: 2. Of those that a mesh axis runs over, the one named last changes fastest.
Arguments:
- seismo: bfloat16 [128, 3, 1173], P(('days', 'sta')), parts along dimension 0, may hold values from -6 to 6
- waves: bfloat16 [4096, 3, 150], P('sta'), may hold values from -6 to 6
- pair_station: int32 [4096, 1], P('sta'), may hold values from 0 to 63; in each aligned block of 256 rows (0 to 255, 256 to 511, ...) at most 8 rows name the same one
- pair_template: int32 [4096], P('sta'), may hold values from 0 to 23, as said below
- chan_mask: int32 [128, 3], P(('days', 'sta')), parts along dimension 0, may hold values from 0 to 1, as said below
Outputs:
- detection: float32 [768, 1024], P(('days', 'sta')), parts along dimension 0
There are 2 independent parts, one for each index of `days`. A program takes and returns all parts, laid end to end along the dimension named above; an argument that names none is the same for every part. Nothing has to cross between parts.
Inputs may be any that keep to these rules, and one draw needn't show every extreme that they name: `pair_station`: within the rows of one device (aligned blocks of 256 rows) no station is named more than 8 times, a bound that some block reaches. `pair_template`: within the rows of one device the numbers never fall and each of the 24 numbers appears at least once. `chan_mask`: every station has at least one available component.
All inputs are finite; a program needn't handle non-finite values.
Results may differ from a plain program's by a relative error of at most 0.0029.
Values may be sent and summed in bfloat16 or wider, within the bound.
A program may use at most 128 MiB of HBM per device.

v0:
```python
import jax
import jax.numpy as jnp
from jax import lax
from jax.sharding import PartitionSpec as P

K_DEV = 24


epsilon = 1e-06


def slot_ranks(stations):
    row_count = stations.shape[-1]
    matched = stations[..., :, None] == stations[..., None, :]
    position = jnp.arange(row_count)
    earlier = position[None, :] < position[:, None]
    return jnp.sum((matched & earlier).astype(jnp.int32), axis=-1)


def masked_scale(seismo, chan_mask, length):
    station_count, comp_count, samples = seismo.shape
    lag_count = samples - length + 1
    squares = jnp.square(seismo.astype(jnp.float32)).reshape(station_count * comp_count, samples)
    sample_pos = jnp.arange(samples)[:, None]
    lag_pos = jnp.arange(lag_count)[None, :]
    band = ((sample_pos >= lag_pos) & (sample_pos < lag_pos + length)).astype(jnp.float32)
    energy = jnp.dot(
        squares, band, precision=lax.Precision.HIGHEST, preferred_element_type=jnp.float32
    )
    energy = energy.reshape(station_count, comp_count, lag_count)
    return chan_mask.astype(jnp.float32)[:, :, None] * lax.rsqrt(energy + epsilon)


def correlate_received(received, seismo, chan_mask):
    local_stations, peer_count, capacity, comp_count, length = received.shape
    samples = seismo.shape[2]
    lag_count = samples - length + 1
    data_scale = masked_scale(seismo, chan_mask, length)
    ordered = jnp.transpose(received, (0, 3, 1, 2, 4))
    wave_energy = jnp.sum(jnp.square(ordered.astype(jnp.float32)), axis=4)
    wave_scale = lax.rsqrt(wave_energy + epsilon)
    filters = ordered.reshape(local_stations * comp_count * peer_count * capacity, 1, length)
    signal = seismo.reshape(1, local_stations * comp_count, samples)
    product = lax.conv_general_dilated(
        signal,
        filters,
        (1,),
        "VALID",
        dimension_numbers=("NCH", "OIH", "NCH"),
        feature_group_count=local_stations * comp_count,
        preferred_element_type=jnp.float32,
    )
    product = product.reshape(local_stations, comp_count, peer_count, capacity, lag_count)
    factor = wave_scale[:, :, :, :, None] * data_scale[:, :, None, None, :]
    return jnp.sum(product * factor, axis=1).astype(jnp.bfloat16)


def per_device(seismo, waves, pair_station, pair_template, chan_mask):
    peer_count = lax.axis_size("sta")
    my_index = lax.axis_index("sta")
    local_stations = seismo.shape[0]
    samples = seismo.shape[2]
    pair_count, comp_count, length = waves.shape
    lag_count = samples - length + 1
    capacity = 2 * pair_count // (local_stations * peer_count)
    station = pair_station[:, 0]
    template_onehot = (pair_template[None, :] == jnp.arange(K_DEV)[:, None]).astype(jnp.bfloat16)
    slot_rank = slot_ranks(station)
    back_slot = (
        station % local_stations * (peer_count * capacity)
        + station // local_stations * capacity
        + slot_rank
    )
    every_wave, every_station = (
        lax.all_gather(waves, "sta", axis=0, tiled=True),
        lax.all_gather(pair_station, "sta", axis=0, tiled=True),
    )
    every_station = every_station.reshape(peer_count, pair_count)
    every_rank = slot_ranks(every_station)
    is_owned = every_station // local_stations == my_index
    local_slot = (every_station - my_index * local_stations) * capacity + every_rank
    local_slot = jnp.where(is_owned, local_slot, -1)
    chooser = (
        local_slot[:, None, :] == jnp.arange(local_stations * capacity)[None, :, None]
    ).astype(jnp.bfloat16)
    chooser = chooser.reshape(peer_count, local_stations, capacity, pair_count)
    every_wave = every_wave.reshape(peer_count, pair_count, comp_count * length)
    received = jnp.einsum(
        "nsrp,npx->snrx", chooser, every_wave, preferred_element_type=jnp.float32
    ).astype(jnp.bfloat16)
    received = received.reshape(local_stations, peer_count, capacity, comp_count, length)
    scores = correlate_received(received, seismo, chan_mask)
    returned = lax.all_to_all(scores, "sta", split_axis=1, concat_axis=1, tiled=True)
    back_onehot = (back_slot[:, None] == jnp.arange(2 * pair_count)[None, :]).astype(jnp.bfloat16)
    combine = jnp.dot(template_onehot, back_onehot, preferred_element_type=jnp.float32).astype(
        jnp.bfloat16
    )
    return jnp.dot(
        combine, returned.reshape(2 * pair_count, lag_count), preferred_element_type=jnp.float32
    )


def solution(mesh):
    return jax.shard_map(
        per_device,
        mesh=mesh,
        in_specs=(
            P(("days", "sta"), None, None),
            P("sta", None, None),
            P("sta", None),
            P("sta"),
            P(("days", "sta"), None),
        ),
        out_specs=P(("days", "sta"), None),
        check_vma=False,
    )
```

profile of v0, /device:TPU:0, one launch (start us, length us, event | category | flops | bytes accessed | tf_op | source)
XLA Modules:
  0.0 195.7 jit_solution(14802406966439224994)
XLA Ops:
  6.5 0.0 all-gather.2.cloned.1.call-start
  6.5 0.7 all-gather.2.cloned.1.call-update
  7.3 0.7 convert_element_type.37
  7.9 0.1 copy.71
  8.0 23.3 %all_gather.6 = s32[4096,1]{0,1:T(1,128)S(1)} all-gather(s32[256,1]{0,1:T(1,128)} %param.7), channel_id=1, replica_groups=mesh['days'=2,'sta'=16] {'sta'}, dimensions={0}, use_global_device_ids=true | all-gather | bytes 17408 | tf_op jit(solution)/shard_map/all_gather | solution.py:76
  31.4 0.5 broadcast.134
  31.9 0.7 reduce.3
  32.6 0.8 copy.62
  33.4 2.1 %fusion.24 = f32[4,3,1024]{2,0,1:T(4,128)S(1)} fusion(s32[1024]{0:T(1024)S(1)} %iota_add_fusion, bf16[4,3,1173]{2,0,1:T(4,128)(2,1)} %param.5, f32[4,3]{0,1:T(4,128)S(1)} %copy.71), kind=kOutput, calls=%fused_computation.20 | convolution fusion | flops 176622080 | bytes 81448 | tf_op jit(solution)/shard_map/dot_general | solution.py:27
  35.5 0.7 copy.67
  36.3 1.3 convert_reduce_fusion
  37.6 25.0 %all-gather.2.cloned.1.call-done = bf16[4096,3,150]{0,2,1:T(8,128)(2,1)} async-done(((bf16[256,3,150]{0,2,1:T(8,128)(2,1)}), bf16[4096,3,150]{0,2,1:T(8,128)(2,1)}) %all-gather.2.cloned.1.call-update) | async-done | bytes 3686416 | tf_op jit(solution)/shard_map/all_gather | solution.py:75
  62.6 5.8 %reshape.105 = bf16[16,256,450]{1,0,2:T(8,128)(2,1)} reshape(bf16[4096,3,150]{0,2,1:T(8,128)(2,1)} %all-gather.2.cloned.1.call-done) | data formatting | bytes 7372800 | tf_op jit(solution)/shard_map/reshape | solution.py:87
  68.4 4.2 %fusion.15 = bf16[4,16,8,450]{3,2,0,1:T(8,128)(2,1)S(1)} fusion(bf16[16,256,450,1]{1,0,2,3:T(8,128)(2,1)} %bitcast.28, s32[4,8]{1,0:T(4,128)S(1)} %multiply_add_fusion, s32[16,256]{1,0:T(8,128)S(1)} %add_select_fusion.1), kind=kOutput, calls=%fused_computation.17 | convolution fusion | flops 118326272 | bytes 4163712 | tf_op jit(solution)/shard_map/nsrp,npx->snrx/dot_general | solution.py:88
  72.5 0.0 copy-start.2
  72.6 0.6 reshape.106
  73.2 0.7 multiply_reduce_fusion.1
  73.9 0.3 copy.69
  74.2 0.1 copy.70
  74.3 0.1 copy.65
  74.4 0.2 copy.66
  74.7 0.0 copy-done.2
  74.7 65.8 %fusion.1 = f32[1,1536,1024]{1,0,2:T(1,128)} fusion(bf16[1,12,1173]{1,0,2:T(2,128)(2,1)S(1)} %copy.67, s32[1536]{0:T(1024)S(1)} %copy-done.2, bf16[1536,150]{0,1:T(8,128)(2,1)S(1)} %copy.66), kind=kOutput, calls=%fused_computation.2 | convolution fusion | flops 5667840000 | bytes 6786552 | tf_op jit(solution)/shard_map/conv_general_dilated | solution.py:44
  140.4 15.8 %copy.68 = f32[1,1536,1024]{2,1,0:T(8,128)} copy(f32[1,1536,1024]{1,0,2:T(1,128)} %fusion.1) | data formatting | bytes 12582912 | tf_op jit(solution)/shard_map/conv_general_dilated | solution.py:44
  156.3 0.0 copy-start
  156.3 3.7 %multiply_reduce_fusion = bf16[4,16,8,1024]{3,2,1,0:T(8,128)(2,1)S(1)} fusion(f32[4,3,16,8,1024]{4,3,2,1,0:T(8,128)} %bitcast.27, f32[4,3,1024]{2,1,0:T(4,128)S(1)} %copy.72, f32[4,3,16,8]{3,2,1,0:T(8,128)S(1)} %copy.70), kind=kLoop, calls=%fused_computation.5 | loop fusion | flops 4194304 | bytes 7395328 | tf_op jit(solution)/shard_map/reduce_sum | solution.py:55
  160.0 0.0 copy-start.1
  160.0 1.1 copy.73
  161.1 3.7 %all-to-all-start = ((bf16[4,16,8,1024]{3,2,0,1:T(8,128)(2,1)}), bf16[4,16,8,1024]{3,2,0,1:T(8,128)(2,1)S(1)}, u32[]{:S(2)}, u32[]{:S(2)}) async-start(bf16[4,16,8,1024]{3,2,0,1:T(8,128)(2,1)} %copy.73), calls=%async_computation | async-start | bytes 2097152 | tf_op jit(solution)/shard_map/all_to_all | solution.py:93
  164.7 0.0 copy-done
  164.7 0.2 convert_reduce_fusion.1
  164.9 22.7 %all-to-all-done = bf16[4,16,8,1024]{3,2,0,1:T(8,128)(2,1)S(1)} async-done(((bf16[4,16,8,1024]{3,2,0,1:T(8,128)(2,1)}), bf16[4,16,8,1024]{3,2,0,1:T(8,128)(2,1)S(1)}, u32[]{:S(2)}, u32[]{:S(2)}) %all-to-all-start) | async-done | bytes 1048608 | tf_op jit(solution)/shard_map/all_to_all | solution.py:93
  187.6 0.1 copy.74
  187.7 0.0 copy-done.1
  187.7 1.1 fusion.27
  (10 shorter events, 0.2 us)
Async XLA Ops:
  6.5 56.1 %all-gather.2.cloned.1.call-start = ((), (), s32[]{:S(2)}) async-start(), calls=%async_computation.1 | async-start | bytes 3969024 | tf_op jit(solution)/shard_map/all_gather | solution.py:75
  72.5 2.1 %copy-start.2 = (s32[1536]{0:T(1024)S(1)}, s32[1536]{0:T(1024)}, u32[]{:S(2)}) copy-start(s32[1536]{0:T(1024)} %constant.55.clone.1) | copy-start | bytes 18436
  156.3 8.5 %copy-start = (s32[256,1]{0,1:T(1,128)S(1)}, s32[256,1]{0,1:T(1,128)}, u32[]{:S(2)}) copy-start(s32[256,1]{0,1:T(1,128)} %param.7) | copy-start | bytes 3076
  160.0 27.7 %copy-start.1 = (s32[256]{0:T(256)S(1)}, s32[256]{0:T(256)}, u32[]{:S(2)}) copy-start(s32[256]{0:T(256)} %param.8) | copy-start | bytes 3076
  161.1 26.6 %all-to-all-start = ((bf16[4,16,8,1024]{3,2,0,1:T(8,128)(2,1)}), bf16[4,16,8,1024]{3,2,0,1:T(8,128)(2,1)S(1)}, u32[]{:S(2)}, u32[]{:S(2)}) async-start(bf16[4,16,8,1024]{3,2,0,1:T(8,128)(2,1)} %copy.73), calls=%async_computation | async-start | bytes 2097152 | tf_op jit(solution)/shard_map/all_to_all | solution.py:93
Sparse Core Ops, SparseCore 0:
  9.5 53.0 all-gather.1
where the time goes:
time: 198 us; the launch traced here: 196 us
  matrix products  73.1 us (37%)
  waiting for transfers between devices  48.4 us (24%)
  local copies, waits for them, and re-layouts  26.2 us (13%)
  blocking collectives  23.3 us (12%)
  between operations  13.6 us (7%)
  other arithmetic  7.36 us (4%)
  starting transfers between devices  3.65 us (2%)
    conv_general_dilated x1, matrix products, correlate_received(): lax.conv_general_dilated(signal, filters, (1,), 'VALID', dimension_number...  65.8 us
    all_gather x1, waiting for transfers between devices, per_device(): lax.all_gather(waves, 'sta', axis=0, tiled=True)  25 us
    all_gather x1, blocking collectives, per_device(): lax.all_gather(pair_station, 'sta', axis=0, tiled=True)  23.3 us
    all_to_all x1, waiting for transfers between devices, per_device(): lax.all_to_all(scores, 'sta', split_axis=1, concat_axis=1, tiled=True)  22.7 us
    conv_general_dilated x1, local copies, waits for them, and re-layouts, correlate_received(): lax.conv_general_dilated(signal, filters, (1,), 'VALID', dimension_number...  15.8 us
    reshape x1, local copies, waits for them, and re-layouts, per_device(): every_wave = every_wave.reshape(peer_count, pair_count, comp_count * length)  5.77 us
    dot_general x1, matrix products, per_device(): jnp.einsum('nsrp,npx->snrx', chooser, every_wave, preferred_element_type=...  4.17 us
  transfers between devices with their start and end apart: 2, of which 2 were waited for; matrix products, arithmetic and copies ran while one was open for 4% of the time, Pallas kernels for 0%

commit v1 on v0

v1 whole, which is shorter than its diff:
```python
import functools

import jax
import jax.numpy as jnp
from jax import lax
from jax.experimental import pallas as pl
from jax.experimental.pallas import tpu as pltpu
from jax.sharding import PartitionSpec as P

K_DEV = 24
SLOTS = 8
PHASES = 8
LANES = 128
WIDE = 256
MESH = pl.DeviceIdType.MESH

epsilon = 1e-06


def dot(a, b):
    return jnp.dot(a, b, preferred_element_type=jnp.float32)


def iota(shape, dim):
    return lax.broadcasted_iota(jnp.int32, shape, dim)


def kernel(
    peers, stations, comps, length,
    seismo_ref, waves_ref, station_ref, template_ref, mask_ref, out_ref,
    got, shifted, chooser, filt, wave_scale, scores, order, send_sem, recv_sem,
):
    f32, bf16 = jnp.float32, jnp.bfloat16
    me = lax.axis_index("sta")
    traces = stations * comps
    samples = seismo_ref.shape[1]
    pairs = waves_ref.shape[0]
    slot_total = peers * stations * SLOTS
    taps = -(-(length + PHASES - 1) // 16) * 16
    steps = taps // PHASES
    per_tail = LANES // steps
    tail_groups = -(-traces // per_tail)
    head_rows = traces * PHASES

    barrier = pltpu.get_barrier_semaphore()

    def greet(i, carry):
        pl.semaphore_signal(
            barrier, inc=1, device_id={"sta": lax.rem(me + i, peers)}, device_id_type=MESH
        )
        return carry

    lax.fori_loop(1, peers, greet, 0)

    pick = (iota((head_rows, traces), 0) // PHASES == iota((head_rows, traces), 1)).astype(f32)
    pick = (pick * mask_ref[...].astype(f32)).astype(bf16)
    spread = dot(pick, seismo_ref[...])
    same_phase = iota((head_rows, samples), 1) % PHASES == iota((head_rows, samples), 0) % PHASES
    spread = jnp.where(same_phase, spread, 0.0).astype(bf16)
    head_pick = (iota((samples, LANES), 0) // PHASES == iota((samples, LANES), 1)).astype(bf16)
    head = dot(spread, head_pick)
    first = PHASES * LANES
    left = samples - first
    tail_pick = (
        iota((left, LANES), 0) // PHASES == iota((left, LANES), 1) % steps
    ).astype(bf16)
    tails = dot(spread[:, first:], tail_pick)
    place = iota((head_rows, LANES), 0) // PHASES % per_tail == iota((head_rows, LANES), 1) // steps
    tails = jnp.where(place, tails, 0.0)
    parts = [head]
    for g in range(tail_groups):
        part = None
        for j in range(g * per_tail, min(traces, (g + 1) * per_tail)):
            one = tails[j * PHASES:(j + 1) * PHASES]
            part = one if part is None else part + one
        parts.append(part)
    if tail_groups % 2:
        parts.append(jnp.zeros((PHASES, LANES), f32))
    got[me] = jnp.concatenate(parts, axis=0).astype(bf16)

    pl.semaphore_wait(barrier, peers - 1)

    def offset(k):
        odd = k % 2
        return odd * ((k + 1) // 2) + (1 - odd) * (peers - k // 2)

    def transfer(k, source):
        return pltpu.make_async_remote_copy(
            src_ref=got.at[source],
            dst_ref=got.at[source],
            send_sem=send_sem.at[k],
            recv_sem=recv_sem.at[source],
            device_id={"sta": lax.rem(me + offset(k), peers)},
            device_id_type=MESH,
        )

    def push(k, carry):
        transfer(k, me).start()
        return carry

    lax.fori_loop(1, peers, push, 0)

    diagonal = iota((pairs, pairs), 0) == iota((pairs, pairs), 1)
    station_column = station_ref[...]
    station_row = jnp.sum(jnp.where(diagonal, station_column, 0), axis=0, keepdims=True)
    earlier = iota((pairs, pairs), 0) < iota((pairs, pairs), 1)
    matched = (station_column == station_row) & earlier
    rank = jnp.sum(matched.astype(jnp.int32), axis=0, keepdims=True)
    slot = station_row * SLOTS + rank
    chooser[...] = (iota((slot_total, pairs), 0) == slot).astype(bf16)

    for c in range(comps):
        lanes = slice(c * WIDE, (c + 1) * WIDE)
        wave = waves_ref[:, lanes].astype(f32)
        for d in range(PHASES):
            moved = wave if d == 0 else pltpu.roll(wave, d, 1)
            shifted[d, :, lanes] = moved.astype(bf16)

    chunk = 128
    blocks = chunk // SLOTS

    def gather(i, carry):
        rows = chooser[pl.ds(pl.multiple_of(i * chunk, chunk), chunk), :]
        for d in range(0, PHASES, 2):
            low = dot(rows, shifted[d])
            high = dot(rows, shifted[d + 1])
            if d == 0:
                for c in range(comps):
                    energy = jnp.sum(
                        jnp.square(low[:, c * WIDE:(c + 1) * WIDE]), axis=1, keepdims=True
                    )
                    wave_scale[
                        pl.ds(pl.multiple_of(i * chunk, chunk), chunk),
                        c * LANES:(c + 1) * LANES,
                    ] = jnp.broadcast_to(lax.rsqrt(energy + epsilon), (chunk, LANES))
            both = jnp.concatenate(
                [low.reshape(blocks, SLOTS, -1), high.reshape(blocks, SLOTS, -1)], axis=1
            )
            filt[pl.ds(i * blocks, blocks), d * SLOTS:(d + 2) * SLOTS, :] = both.astype(bf16)
        return carry

    lax.fori_loop(0, slot_total // chunk, gather, 0)

    tap, phase = iota((16, taps), 1), iota((16, taps), 0)
    band = ((tap >= phase) & (tap < phase + length)).astype(bf16)
    lane = iota((PHASES, LANES), 1)

    def correlate(k, carry):
        peer = lax.rem(me + 2 * peers - offset(k), peers)

        @pl.when(k > 0)
        def _():
            transfer(k, peer).wait_recv()

        block = got[peer].astype(f32)

        def one_station(s):
            total = None
            for c in range(comps):
                j = s * comps + c
                head = block[j * PHASES:(j + 1) * PHASES]
                group = head_rows + j // per_tail * PHASES
                tail = block[group:group + PHASES]
                rows = [head]
                for q in range(1, steps):
                    begin = pltpu.roll(head, LANES - q, 1)
                    end = pltpu.roll(tail, (LANES - q - steps * (j % per_tail)) % LANES, 1)
                    rows.append(jnp.where(lane < LANES - q, begin, end))
                data = jnp.concatenate(rows, axis=0).astype(bf16)
                product = dot(filt[peer * stations + s, :, c * WIDE:c * WIDE + taps], data)
                energy = dot(band, data * data)[:PHASES]
                data_scale = lax.rsqrt(energy + epsilon)
                start = pl.multiple_of((peer * stations + s) * SLOTS, SLOTS)
                scale = wave_scale[pl.ds(start, SLOTS), c * LANES:(c + 1) * LANES]
                factor = data_scale[:, None, :] * scale[None, :, :]
                term = product.reshape(PHASES, SLOTS, LANES) * factor
                total = term if total is None else total + term
            return total

        for s in range(0, stations, 2):
            low, high = one_station(s), one_station(s + 1)
            start = pl.multiple_of((peer * stations + s) * SLOTS, 2 * SLOTS)
            for d in range(PHASES):
                scores[pl.ds(start, 2 * SLOTS), d * LANES:(d + 1) * LANES] = jnp.concatenate(
                    [low[d], high[d]], axis=0
                ).astype(bf16)
        return carry

    lax.fori_loop(0, peers, correlate, 0)

    lags = PHASES * LANES
    for d in range(PHASES):
        order[d * LANES:(d + 1) * LANES, :] = (
            iota((LANES, lags), 1) == PHASES * iota((LANES, lags), 0) + d
        ).astype(bf16)
    member = (iota((32, pairs), 0) == template_ref[...]).astype(bf16)
    combine = lax.dot_general(
        member, chooser[...], (((1,), (1,)), ((), ())), preferred_element_type=f32
    ).astype(bf16)
    found = dot(combine, scores[...])
    coarse = found.astype(bf16)
    fine = (found - coarse.astype(f32)).astype(bf16)
    out = dot(coarse, order[...]) + dot(fine, order[...])
    out_ref[...] = out[:K_DEV]

    def drain(k, carry):
        transfer(k, me).wait_send()
        return carry

    lax.fori_loop(1, peers, drain, 0)


def per_device(peers, seismo, waves, pair_station, pair_template, chan_mask):
    stations, comps, samples = seismo.shape
    pairs, _, length = waves.shape
    lags = samples - length + 1
    assert lags == PHASES * LANES
    assert 2 * pairs // (stations * peers) <= SLOTS
    slot_total = peers * stations * SLOTS
    steps = -(-(length + PHASES - 1) // 16) * 16 // PHASES
    tail_groups = -(-stations * comps // (LANES // steps))
    rows = -(-(stations * comps + tail_groups) // 2) * 2 * PHASES
    wide = jnp.pad(waves, ((0, 0), (0, 0), (0, WIDE - length))).reshape(pairs, comps * WIDE)
    vmem = pl.BlockSpec(memory_space=pltpu.VMEM)
    bf16 = jnp.bfloat16
    return pl.pallas_call(
        functools.partial(kernel, peers, stations, comps, length),
        out_shape=jax.ShapeDtypeStruct((K_DEV, lags), jnp.float32),
        in_specs=[vmem] * 5,
        out_specs=vmem,
        scratch_shapes=[
            pltpu.VMEM((peers, rows, LANES), bf16),
            pltpu.VMEM((PHASES, pairs, comps * WIDE), bf16),
            pltpu.VMEM((slot_total, pairs), bf16),
            pltpu.VMEM((peers * stations, PHASES * SLOTS, comps * WIDE), bf16),
            pltpu.VMEM((slot_total, comps * LANES), jnp.float32),
            pltpu.VMEM((slot_total, lags), bf16),
            pltpu.VMEM((lags, lags), bf16),
            pltpu.SemaphoreType.DMA((peers,)),
            pltpu.SemaphoreType.DMA((peers,)),
        ],
        compiler_params=pltpu.CompilerParams(
            collective_id=0, has_side_effects=True, vmem_limit_bytes=56 * 1024 * 1024
        ),
    )(
        seismo.reshape(stations * comps, samples),
        wide,
        pair_station,
        pair_template.reshape(1, pairs),
        chan_mask.reshape(1, stations * comps),
    )


def solution(mesh):
    return jax.shard_map(
        functools.partial(per_device, mesh.shape["sta"]),
        mesh=mesh,
        in_specs=(
            P(("days", "sta"), None, None),
            P("sta", None, None),
            P("sta", None),
            P("sta"),
            P(("days", "sta"), None),
        ),
        out_specs=P(("days", "sta"), None),
        check_vma=False,
    )
```

time: 198 us -> 29 us (0.15); the launches traced: 196 us -> 28.8 us
  matrix products: 73.1 us -> 0 us
  waiting for transfers between devices: 48.4 us -> 0 us
  blocking collectives: 23.3 us -> 0 us
  Pallas kernels: 0 us -> 23.2 us
  local copies, waits for them, and re-layouts: 26.2 us -> 5.58 us
  between operations: 13.6 us -> 0.04 us
  other arithmetic: 7.36 us -> 0 us
  starting transfers between devices: 3.65 us -> 0 us
    conv_general_dilated x1 -> x0, matrix products: 65.8 us -> none  [correlate_received(): lax.conv_general_dilated(signal, filters, (1,), 'VALID', dimension_number...]
    all_gather x1 -> x0, waiting for transfers between devices: 25 us -> none  [per_device(): lax.all_gather(waves, 'sta', axis=0, tiled=True)]
    all_gather x1 -> x0, blocking collectives: 23.3 us -> none  [per_device(): lax.all_gather(pair_station, 'sta', axis=0, tiled=True)]
    pallas_call x0 -> x1, Pallas kernels: none -> 23.2 us  [per_device(): pl.pallas_call(functools.partial(kernel, peers, stations, comps, length),...]
    all_to_all x1 -> x0, waiting for transfers between devices: 22.7 us -> none  [per_device(): lax.all_to_all(scores, 'sta', split_axis=1, concat_axis=1, tiled=True)]
    conv_general_dilated x1 -> x0, local copies, waits for them, and re-layouts: 15.8 us -> none  [correlate_received(): lax.conv_general_dilated(signal, filters, (1,), 'VALID', dimension_number...]
    dot_general x3 -> x0, matrix products: 7.37 us -> none  [the longest x1 4.17 us: per_device(): jnp.einsum('nsrp,npx->snrx', chooser, every_wave, preferred_element_type=...]
    reduce_sum x4 -> x0, other arithmetic: 5.89 us -> none  [the longest x1 3.73 us: correlate_received(): return jnp.sum(product * factor, axis=1).astype(jnp.bfloat16)]
  transfers between devices with their start and end apart: 2 -> 0, of which waited for: 2 -> 0; matrix products, arithmetic and copies ran while one was open for 4% -> 0% of each run, Pallas kernels for 0% -> 0%
where the time goes in v1:
time: 29 us; the launch traced here: 28.8 us
  Pallas kernels  23.2 us (80%)
  local copies, waits for them, and re-layouts  5.58 us (19%)
    pallas_call x1, Pallas kernels, per_device(): pl.pallas_call(functools.partial(kernel, peers, stations, comps, length),...  23.2 us
    unnamed x9, local copies, waits for them, and re-layouts  2.39 us
    pad x1, local copies, waits for them, and re-layouts, per_device(): jnp.pad(waves, ((0, 0), (0, 0), (0, WIDE - length)))  0.97 us
    reshape x1, local copies, waits for them, and re-layouts, per_device(): jnp.pad(waves, ((0, 0), (0, 0), (0, WIDE - length)))  0.93 us
    reshape x1, local copies, waits for them, and re-layouts, per_device(): seismo.reshape(stations * comps, samples)  0.65 us
    reshape x1, local copies, waits for them, and re-layouts, per_device(): chan_mask.reshape(1, stations * comps)  0.65 us

profile of v1, /device:TPU:0, one launch (start us, length us, event | category | flops | bytes accessed | tf_op | source)
XLA Modules:
  0.0 28.8 jit_solution(9774855456092403379)
XLA Ops:
  0.0 1.0 %pad.4 = bf16[256,3,256]{0,2,1:T(8,128)(2,1)S(1)} pad(bf16[256,3,150]{0,2,1:T(8,128)(2,1)} %param.6, bf16[]{:T(256)} %constant.2.clone.1), padding=0_0x0_0x0_106 | pad | bytes 623618 | tf_op jit(solution)/shard_map/jit(_pad)/pad | solution.py:223
  1.0 0.0 copy-start.2
  1.0 0.9 %copy.10.waves_ref = bf16[256,768]{1,0:T(8,128)(2,1)} copy(bf16[256,768]{0,1:T(8,128)(2,1)S(1)} %bitcast.2) | data formatting | bytes 786432 | tf_op jit(solution)/shard_map/reshape | solution.py:223
  1.9 0.0 copy-done.2
  1.9 0.0 copy-start
  1.9 0.8 %copy.11.station_ref = s32[256,1]{1,0:T(8,128)} copy(s32[256,1]{0,1:T(1,128)S(1)} %copy-done.2) | data formatting | bytes 2048 | tf_op args[2]
  2.7 0.0 copy-done
  2.7 0.0 copy-start.1
  2.8 0.7 %reshape.12.seismo_ref = bf16[12,1173]{1,0:T(8,128)(2,1)} reshape(bf16[4,3,1173]{2,1,0:T(4,128)(2,1)S(1)} %copy.9) | data formatting | bytes 56304 | tf_op jit(solution)/shard_map/reshape | solution.py:246
  3.4 0.0 copy-done.1
  3.4 0.6 %reshape.15.mask_ref = s32[1,12]{1,0:T(1,128)} reshape(s32[4,3]{1,0:T(4,128)S(1)} %copy-done.1) | data formatting | bytes 96 | tf_op jit(solution)/shard_map/reshape | solution.py:250
  4.1 23.2 %shard_map.55 = f32[24,1024]{1,0:T(8,128)} custom-call(bf16[12,1173]{1,0:T(8,128)(2,1)} %reshape.12.seismo_ref, bf16[256,768]{1,0:T(8,128)(2,1)} %copy.10.waves_ref, s32[256,1]{1,0:T(8,128)} %copy.11.station_ref, s32[1,256]{1,0:T(1,128)} %bitcast.3, s32[1,12]{1,0:T(1,128)} %reshape.15.mask_ref), custom_call_target="tpu_custom_call" | custom-call | tf_op jit(solution)/shard_map/pallas_call | solution.py:226
  27.2 1.5 %copy.13 = f32[24,1024]{1,0:T(8,128)} copy(f32[24,1024]{1,0:T(8,128)} %shard_map.55) | data formatting | bytes 196608
  (1 shorter events, 0.0 us)
Async XLA Ops:
  1.0 0.9 %copy-start.2 = (s32[256,1]{0,1:T(1,128)S(1)}, s32[256,1]{0,1:T(1,128)}, u32[]{:S(2)}) copy-start(s32[256,1]{0,1:T(1,128)} %param.7) | copy-start | bytes 3076
  1.9 0.8 %copy-start = (bf16[4,3,1173]{2,0,1:T(4,128)(2,1)S(1)}, bf16[4,3,1173]{2,0,1:T(4,128)(2,1)}, u32[]{:S(2)}) copy-start(bf16[4,3,1173]{2,0,1:T(4,128)(2,1)} %param.5) | copy-start | bytes 84460
  2.7 0.7 %copy-start.1 = (s32[4,3]{1,0:T(4,128)S(1)}, s32[4,3]{1,0:T(4,128)}, u32[]{:S(2)}) copy-start(s32[4,3]{1,0:T(4,128)} %param.9) | copy-start | bytes 148

commit v2 on v1

--- a/solution.py
+++ b/solution.py
@@ -33,8 +33,8 @@
     f32, bf16 = jnp.float32, jnp.bfloat16
     me = lax.axis_index("sta")
     traces = stations * comps
-    samples = seismo_ref.shape[1]
-    pairs = waves_ref.shape[0]
+    samples = seismo_ref.shape[2]
+    pairs = waves_ref.shape[2]
     slot_total = peers * stations * SLOTS
     taps = -(-(length + PHASES - 1) // 16) * 16
     steps = taps // PHASES
@@ -52,9 +52,13 @@
 
     lax.fori_loop(1, peers, greet, 0)
 
-    pick = (iota((head_rows, traces), 0) // PHASES == iota((head_rows, traces), 1)).astype(f32)
-    pick = (pick * mask_ref[...].astype(f32)).astype(bf16)
-    spread = dot(pick, seismo_ref[...])
+    spread = None
+    for c in range(comps):
+        source = iota((head_rows, stations), 0) // PHASES
+        pick = (source == iota((head_rows, stations), 1) * comps + c).astype(bf16)
+        record = seismo_ref[c].astype(f32) * mask_ref[:, c:c + 1].astype(f32)
+        one = dot(pick, record.astype(bf16))
+        spread = one if spread is None else spread + one
     same_phase = iota((head_rows, samples), 1) % PHASES == iota((head_rows, samples), 0) % PHASES
     spread = jnp.where(same_phase, spread, 0.0).astype(bf16)
     head_pick = (iota((samples, LANES), 0) // PHASES == iota((samples, LANES), 1)).astype(bf16)
@@ -101,8 +105,8 @@
     lax.fori_loop(1, peers, push, 0)
 
     diagonal = iota((pairs, pairs), 0) == iota((pairs, pairs), 1)
-    station_column = station_ref[...]
-    station_row = jnp.sum(jnp.where(diagonal, station_column, 0), axis=0, keepdims=True)
+    station_row = station_ref[...]
+    station_column = jnp.sum(jnp.where(diagonal, station_row, 0), axis=1, keepdims=True)
     earlier = iota((pairs, pairs), 0) < iota((pairs, pairs), 1)
     matched = (station_column == station_row) & earlier
     rank = jnp.sum(matched.astype(jnp.int32), axis=0, keepdims=True)
@@ -110,33 +114,40 @@
     chooser[...] = (iota((slot_total, pairs), 0) == slot).astype(bf16)
 
     for c in range(comps):
-        lanes = slice(c * WIDE, (c + 1) * WIDE)
-        wave = waves_ref[:, lanes].astype(f32)
+        wave = jnp.concatenate(
+            [waves_ref[c].astype(f32), jnp.zeros((taps - length, pairs), f32)], axis=0
+        )
         for d in range(PHASES):
-            moved = wave if d == 0 else pltpu.roll(wave, d, 1)
-            shifted[d, :, lanes] = moved.astype(bf16)
+            moved = wave if d == 0 else pltpu.roll(wave, d, 0)
+            shifted[d, c] = moved.astype(bf16)
 
     chunk = 128
     blocks = chunk // SLOTS
 
     def gather(i, carry):
-        rows = chooser[pl.ds(pl.multiple_of(i * chunk, chunk), chunk), :]
-        for d in range(0, PHASES, 2):
-            low = dot(rows, shifted[d])
-            high = dot(rows, shifted[d + 1])
-            if d == 0:
-                for c in range(comps):
-                    energy = jnp.sum(
-                        jnp.square(low[:, c * WIDE:(c + 1) * WIDE]), axis=1, keepdims=True
+        span = pl.ds(pl.multiple_of(i * chunk, chunk), chunk)
+        rows = chooser[span, :]
+        for c in range(comps):
+            for d in range(0, PHASES, 2):
+                low, high = [
+                    lax.dot_general(
+                        rows, shifted[d + e, c], (((1,), (1,)), ((), ())),
+                        preferred_element_type=f32,
                     )
-                    wave_scale[
-                        pl.ds(pl.multiple_of(i * chunk, chunk), chunk),
-                        c * LANES:(c + 1) * LANES,
-                    ] = jnp.broadcast_to(lax.rsqrt(energy + epsilon), (chunk, LANES))
-            both = jnp.concatenate(
-                [low.reshape(blocks, SLOTS, -1), high.reshape(blocks, SLOTS, -1)], axis=1
-            )
-            filt[pl.ds(i * blocks, blocks), d * SLOTS:(d + 2) * SLOTS, :] = both.astype(bf16)
+                    for e in range(2)
+                ]
+                if d == 0:
+                    energy = jnp.sum(jnp.square(low), axis=1, keepdims=True)
+                    wave_scale[span, c * LANES:(c + 1) * LANES] = jnp.broadcast_to(
+                        lax.rsqrt(energy + epsilon), (chunk, LANES)
+                    )
+                both = jnp.concatenate(
+                    [low.reshape(blocks, SLOTS, taps), high.reshape(blocks, SLOTS, taps)], axis=1
+                )
+                filt[
+                    pl.ds(i * blocks, blocks), d * SLOTS:(d + 2) * SLOTS,
+                    c * WIDE:c * WIDE + taps,
+                ] = both.astype(bf16)
         return carry
 
     lax.fori_loop(0, slot_total // chunk, gather, 0)
@@ -220,7 +231,6 @@
     steps = -(-(length + PHASES - 1) // 16) * 16 // PHASES
     tail_groups = -(-stations * comps // (LANES // steps))
     rows = -(-(stations * comps + tail_groups) // 2) * 2 * PHASES
-    wide = jnp.pad(waves, ((0, 0), (0, 0), (0, WIDE - length))).reshape(pairs, comps * WIDE)
     vmem = pl.BlockSpec(memory_space=pltpu.VMEM)
     bf16 = jnp.bfloat16
     return pl.pallas_call(
@@ -230,7 +240,7 @@
         out_specs=vmem,
         scratch_shapes=[
             pltpu.VMEM((peers, rows, LANES), bf16),
-            pltpu.VMEM((PHASES, pairs, comps * WIDE), bf16),
+            pltpu.VMEM((PHASES, comps, steps * PHASES, pairs), bf16),
             pltpu.VMEM((slot_total, pairs), bf16),
             pltpu.VMEM((peers * stations, PHASES * SLOTS, comps * WIDE), bf16),
             pltpu.VMEM((slot_total, comps * LANES), jnp.float32),
@@ -243,11 +253,11 @@
             collective_id=0, has_side_effects=True, vmem_limit_bytes=56 * 1024 * 1024
         ),
     )(
-        seismo.reshape(stations * comps, samples),
-        wide,
-        pair_station,
+        jnp.transpose(seismo, (1, 0, 2)),
+        jnp.transpose(waves, (1, 2, 0)),
+        pair_station.reshape(1, pairs),
         pair_template.reshape(1, pairs),
-        chan_mask.reshape(1, stations * comps),
+        chan_mask,
     )
 
 

time: 29 us -> 25 us (0.86)
  local copies, waits for them, and re-layouts: 5.58 us -> 1.54 us
    reshape x3 -> x0, local copies, waits for them, and re-layouts: 2.23 us -> none  [the longest x1 0.93 us: per_device(): jnp.pad(waves, ((0, 0), (0, 0), (0, WIDE - length)))]
    pad x1 -> x0, local copies, waits for them, and re-layouts: 0.97 us -> none  [per_device(): jnp.pad(waves, ((0, 0), (0, 0), (0, WIDE - length)))]
    unnamed x9 -> x1, local copies, waits for them, and re-layouts: 2.39 us -> 1.54 us
where the time goes in v2:
time: 25 us; the launch traced here: 24.8 us
  Pallas kernels  23.3 us (93%)
  local copies, waits for them, and re-layouts  1.54 us (6%)
    pallas_call x1, Pallas kernels, per_device(): pl.pallas_call(functools.partial(kernel, peers, stations, comps, length),...  23.3 us
    unnamed x1, local copies, waits for them, and re-layouts  1.54 us

profile of v2, /device:TPU:0, one launch (start us, length us, event | category | flops | bytes accessed | tf_op | source)
XLA Modules:
  0.0 24.8 jit_solution(12825686426524188397)
XLA Ops:
  0.0 23.3 %shard_map.55 = f32[24,1024]{1,0:T(8,128)} custom-call(bf16[3,4,1173]{2,1,0:T(4,128)(2,1)} %bitcast.5, bf16[3,150,256]{2,1,0:T(8,128)(2,1)} %bitcast.4, s32[1,256]{1,0:T(1,128)} %bitcast.6, s32[1,256]{1,0:T(1,128)} %bitcast.7, s32[4,3]{1,0:T(4,128)} %mask_ref.1), custom_call_target="tpu_custom_call" | custom-call | tf_op jit(solution)/shard_map/pallas_call | solution.py:236
  23.3 1.5 %copy.7 = f32[24,1024]{1,0:T(8,128)} copy(f32[24,1024]{1,0:T(8,128)} %shard_map.55) | data formatting | bytes 196608

commit v3 on v2

--- a/solution.py
+++ b/solution.py
@@ -82,8 +82,6 @@
         parts.append(jnp.zeros((PHASES, LANES), f32))
     got[me] = jnp.concatenate(parts, axis=0).astype(bf16)
 
-    pl.semaphore_wait(barrier, peers - 1)
-
     def offset(k):
         odd = k % 2
         return odd * ((k + 1) // 2) + (1 - odd) * (peers - k // 2)
@@ -98,12 +96,6 @@
             device_id_type=MESH,
         )
 
-    def push(k, carry):
-        transfer(k, me).start()
-        return carry
-
-    lax.fori_loop(1, peers, push, 0)
-
     diagonal = iota((pairs, pairs), 0) == iota((pairs, pairs), 1)
     station_row = station_ref[...]
     station_column = jnp.sum(jnp.where(diagonal, station_row, 0), axis=1, keepdims=True)
@@ -121,7 +113,24 @@
             moved = wave if d == 0 else pltpu.roll(wave, d, 0)
             shifted[d, c] = moved.astype(bf16)
 
-    chunk = 128
+    lags = PHASES * LANES
+    for d in range(PHASES):
+        order[d * LANES:(d + 1) * LANES, :] = (
+            iota((LANES, lags), 1) == PHASES * iota((LANES, lags), 0) + d
+        ).astype(bf16)
+    member = (iota((32, pairs), 0) == template_ref[...]).astype(bf16)
+    combine = lax.dot_general(
+        member, chooser[...], (((1,), (1,)), ((), ())), preferred_element_type=f32
+    ).astype(bf16)
+    pl.semaphore_wait(barrier, peers - 1)
+
+    def push(k, carry):
+        transfer(k, me).start()
+        return carry
+
+    lax.fori_loop(1, peers, push, 0)
+
+    chunk = min(2 * pairs, slot_total)
     blocks = chunk // SLOTS
 
     def gather(i, carry):
@@ -165,31 +174,39 @@
 
         block = got[peer].astype(f32)
 
-        def one_station(s):
-            total = None
-            for c in range(comps):
-                j = s * comps + c
-                head = block[j * PHASES:(j + 1) * PHASES]
-                group = head_rows + j // per_tail * PHASES
-                tail = block[group:group + PHASES]
-                rows = [head]
-                for q in range(1, steps):
-                    begin = pltpu.roll(head, LANES - q, 1)
-                    end = pltpu.roll(tail, (LANES - q - steps * (j % per_tail)) % LANES, 1)
-                    rows.append(jnp.where(lane < LANES - q, begin, end))
-                data = jnp.concatenate(rows, axis=0).astype(bf16)
-                product = dot(filt[peer * stations + s, :, c * WIDE:c * WIDE + taps], data)
-                energy = dot(band, data * data)[:PHASES]
-                data_scale = lax.rsqrt(energy + epsilon)
-                start = pl.multiple_of((peer * stations + s) * SLOTS, SLOTS)
-                scale = wave_scale[pl.ds(start, SLOTS), c * LANES:(c + 1) * LANES]
-                factor = data_scale[:, None, :] * scale[None, :, :]
-                term = product.reshape(PHASES, SLOTS, LANES) * factor
-                total = term if total is None else total + term
-            return total
+        def windows(j):
+            head = block[j * PHASES:(j + 1) * PHASES]
+            group = head_rows + j // per_tail * PHASES
+            tail = block[group:group + PHASES]
+            rows = [head]
+            for q in range(1, steps):
+                begin = pltpu.roll(head, LANES - q, 1)
+                end = pltpu.roll(tail, (LANES - q - steps * (j % per_tail)) % LANES, 1)
+                rows.append(jnp.where(lane < LANES - q, begin, end))
+            return jnp.concatenate(rows, axis=0).astype(bf16)
+
+        def two_stations(s):
+            data = [windows(j) for j in range(s * comps, (s + 2) * comps)]
+            squares = jnp.concatenate([x * x for x in data], axis=1)
+            data_scale = lax.rsqrt(dot(band, squares)[:PHASES] + epsilon)
+            totals = []
+            for e in range(2):
+                total = None
+                for c in range(comps):
+                    j = e * comps + c
+                    rows = filt[peer * stations + s + e, :, c * WIDE:c * WIDE + taps]
+                    product = dot(rows, data[j])
+                    start = pl.multiple_of((peer * stations + s + e) * SLOTS, SLOTS)
+                    scale = wave_scale[pl.ds(start, SLOTS), c * LANES:(c + 1) * LANES]
+                    own = data_scale[:, j * LANES:(j + 1) * LANES]
+                    factor = own[:, None, :] * scale[None, :, :]
+                    term = product.reshape(PHASES, SLOTS, LANES) * factor
+                    total = term if total is None else total + term
+                totals.append(total)
+            return totals
 
         for s in range(0, stations, 2):
-            low, high = one_station(s), one_station(s + 1)
+            low, high = two_stations(s)
             start = pl.multiple_of((peer * stations + s) * SLOTS, 2 * SLOTS)
             for d in range(PHASES):
                 scores[pl.ds(start, 2 * SLOTS), d * LANES:(d + 1) * LANES] = jnp.concatenate(
@@ -199,15 +216,6 @@
 
     lax.fori_loop(0, peers, correlate, 0)
 
-    lags = PHASES * LANES
-    for d in range(PHASES):
-        order[d * LANES:(d + 1) * LANES, :] = (
-            iota((LANES, lags), 1) == PHASES * iota((LANES, lags), 0) + d
-        ).astype(bf16)
-    member = (iota((32, pairs), 0) == template_ref[...]).astype(bf16)
-    combine = lax.dot_general(
-        member, chooser[...], (((1,), (1,)), ((), ())), preferred_element_type=f32
-    ).astype(bf16)
     found = dot(combine, scores[...])
     coarse = found.astype(bf16)
     fine = (found - coarse.astype(f32)).astype(bf16)

time: 25 us -> 22.9 us (0.916); the launches traced: 24.8 us -> 22.5 us
  Pallas kernels: 23.3 us -> 20.9 us
    pallas_call x1, Pallas kernels: 23.3 us -> 20.9 us  [per_device(): pl.pallas_call(functools.partial(kernel, peers, stations, comps, length),...]
where the time goes in v3:
time: 22.9 us; the launch traced here: 22.5 us
  Pallas kernels  20.9 us (91%)
  local copies, waits for them, and re-layouts  1.54 us (7%)
    pallas_call x1, Pallas kernels, per_device(): pl.pallas_call(functools.partial(kernel, peers, stations, comps, length),...  20.9 us
    unnamed x1, local copies, waits for them, and re-layouts  1.54 us

profile of v3, /device:TPU:0, one launch (start us, length us, event | category | flops | bytes accessed | tf_op | source)
XLA Modules:
  0.0 22.5 jit_solution(3020815371715058436)
XLA Ops:
  0.0 20.9 %shard_map.55 = f32[24,1024]{1,0:T(8,128)} custom-call(bf16[3,4,1173]{2,1,0:T(4,128)(2,1)} %bitcast.5, bf16[3,150,256]{2,1,0:T(8,128)(2,1)} %bitcast.4, s32[1,256]{1,0:T(1,128)} %bitcast.6, s32[1,256]{1,0:T(1,128)} %bitcast.7, s32[4,3]{1,0:T(4,128)} %mask_ref.1), custom_call_target="tpu_custom_call" | custom-call | tf_op jit(solution)/shard_map/pallas_call | solution.py:244
  20.9 1.5 %copy.7 = f32[24,1024]{1,0:T(8,128)} copy(f32[24,1024]{1,0:T(8,128)} %shard_map.55) | data formatting | bytes 196608

commit v4 on v3

--- a/solution.py
+++ b/solution.py
@@ -82,9 +82,15 @@
         parts.append(jnp.zeros((PHASES, LANES), f32))
     got[me] = jnp.concatenate(parts, axis=0).astype(bf16)
 
-    def offset(k):
-        odd = k % 2
-        return odd * ((k + 1) // 2) + (1 - odd) * (peers - k // 2)
+    assert peers & (peers - 1) == 0
+
+    def partner(k):
+        total = 0
+        bit = 1
+        while bit < peers:
+            total = total + (me // bit + k // bit) % 2 * bit
+            bit *= 2
+        return total
 
     def transfer(k, source):
         return pltpu.make_async_remote_copy(
@@ -92,7 +98,7 @@
             dst_ref=got.at[source],
             send_sem=send_sem.at[k],
             recv_sem=recv_sem.at[source],
-            device_id={"sta": lax.rem(me + offset(k), peers)},
+            device_id={"sta": partner(k)},
             device_id_type=MESH,
         )
 
@@ -166,7 +172,7 @@
     lane = iota((PHASES, LANES), 1)
 
     def correlate(k, carry):
-        peer = lax.rem(me + 2 * peers - offset(k), peers)
+        peer = partner(k)
 
         @pl.when(k > 0)
         def _():

time: 22.9 us -> 22.6 us (0.987); the launches traced: 22.5 us -> 22.5 us
  no operation moved by 1% of the time
where the time goes in v4:
time: 22.6 us; the launch traced here: 22.5 us
  Pallas kernels  20.9 us (92%)
  local copies, waits for them, and re-layouts  1.54 us (7%)
    pallas_call x1, Pallas kernels, per_device(): pl.pallas_call(functools.partial(kernel, peers, stations, comps, length),...  20.9 us
    unnamed x1, local copies, waits for them, and re-layouts  1.54 us

profile of v4, /device:TPU:0, one launch (start us, length us, event | category | flops | bytes accessed | tf_op | source)
XLA Modules:
  0.0 22.5 jit_solution(5891914667525116645)
XLA Ops:
  0.0 20.9 %shard_map.55 = f32[24,1024]{1,0:T(8,128)} custom-call(bf16[3,4,1173]{2,1,0:T(4,128)(2,1)} %bitcast.5, bf16[3,150,256]{2,1,0:T(8,128)(2,1)} %bitcast.4, s32[1,256]{1,0:T(1,128)} %bitcast.6, s32[1,256]{1,0:T(1,128)} %bitcast.7, s32[4,3]{1,0:T(4,128)} %mask_ref.1), custom_call_target="tpu_custom_call" | custom-call | tf_op jit(solution)/shard_map/pallas_call | solution.py:250
  21.0 1.5 %copy.7 = f32[24,1024]{1,0:T(8,128)} copy(f32[24,1024]{1,0:T(8,128)} %shard_map.55) | data formatting | bytes 196608
